TPU v7x, 32 devices: a whole 2x2x4 slice. The times are simulated.
32 devices in a mesh: row: 8 (over z, core), col: 4 (over y, x).
Axes of the slice: x: 2, y: 2, z: 4, core: 2. Of those that a mesh axis runs over, the one named last changes fastest.
Arguments:
- tokens: bfloat16 [512, 12288], P('col', 'row'), may hold values from -6 to 6
- weight_in: bfloat16 [12288, 24576], P('row', 'col'), may hold values from -0.0546875 to 0.0546875
- weight_out: bfloat16 [24576, 12288], P('col', 'row'), may hold values from -0.0390625 to 0.0390625
- bias_in: bfloat16 [24576], P('col'), may hold values from -3 to 3
- cotangent: bfloat16 [512, 12288], P('col', 'row'), may hold values from -6 to 6
Outputs:
- output: bfloat16 [512, 12288], P('col', 'row')
- grad_tokens: bfloat16 [512, 12288], P('col', 'row')
- grad_weight_in: bfloat16 [12288, 24576], P('row', 'col')
- grad_weight_out: bfloat16 [24576, 12288], P('col', 'row')
- grad_bias: float32 [24576], P('col')
All inputs are finite; a program needn't handle non-finite values.
Results may differ from a plain program's by a relative error of at most 0.03.
Values may be sent and summed in bfloat16 or wider, within the bound.
A program may use at most 192 MiB of HBM per device.

v0:
```python
import math

import jax
import jax.numpy as jnp
from jax import lax
from jax.sharding import PartitionSpec as P

gelu_coef = math.sqrt(2.0 / math.pi)
cubic_coef = 0.044715


def gelu_tanh(values):
    inner = jnp.tanh(gelu_coef * (values + cubic_coef * values * values * values))
    return 0.5 * values * (1.0 + inner)


def gelu_slope(values):
    inner = jnp.tanh(gelu_coef * (values + cubic_coef * values * values * values))
    return 0.5 * (1.0 + inner) + 0.5 * values * (1.0 - inner * inner) * gelu_coef * (
        1.0 + 3.0 * cubic_coef * values * values
    )


def rounded(values):
    return values.astype(jnp.bfloat16).astype(jnp.float32)


def times_transposed(left, right):
    return lax.dot_general(
        left, right, (((1,), (1,)), ((), ())), preferred_element_type=jnp.float32
    )


def over_tokens(left, right):
    return lax.dot_general(
        left, right, (((0,), (0,)), ((), ())), preferred_element_type=jnp.float32
    )


def per_device(tokens, weight_in, weight_out, bias_in, cotangent):
    rows_here = tokens.shape[0]
    total_rows = rows_here * lax.axis_size("col")
    factor = 1.0 / math.sqrt(total_rows)
    bias_wide = bias_in.astype(jnp.float32)
    tokens_all = lax.all_gather(tokens, "col", axis=0, tiled=True)
    sliced = tokens_all
    pre_gelu = (
        lax.psum_scatter(
            rounded(jnp.dot(sliced, weight_in, preferred_element_type=jnp.float32)).astype(
                jnp.bfloat16
            ),
            "row",
            scatter_dimension=0,
            tiled=True,
        ).astype(jnp.float32)
        + bias_wide
    )
    hidden = gelu_tanh(pre_gelu).astype(jnp.bfloat16)
    hidden_all = lax.all_gather(hidden, "row", axis=0, tiled=True)
    sliced = hidden_all
    output = lax.psum_scatter(
        rounded(jnp.dot(sliced, weight_out, preferred_element_type=jnp.float32)).astype(
            jnp.bfloat16
        ),
        "col",
        scatter_dimension=0,
        tiled=True,
    )
    cotangent_all = lax.all_gather(cotangent, "col", axis=0, tiled=True)
    sliced = cotangent_all
    back_grad = lax.psum_scatter(
        rounded(times_transposed(sliced, weight_out)).astype(jnp.bfloat16),
        "row",
        scatter_dimension=0,
        tiled=True,
    ).astype(jnp.float32)
    slope_grad = (back_grad * gelu_slope(pre_gelu)).astype(jnp.bfloat16)
    slope_all = lax.all_gather(slope_grad, "row", axis=0, tiled=True)
    grad_weight_out = (over_tokens(hidden_all, cotangent_all) * factor).astype(jnp.bfloat16)
    grad_weight_in = (over_tokens(tokens_all, slope_all) * factor).astype(jnp.bfloat16)
    grad_bias = jnp.sum(slope_all, axis=0, dtype=jnp.float32) * factor
    sliced = slope_all
    grad_tokens = lax.psum_scatter(
        rounded(times_transposed(sliced, weight_in)).astype(jnp.bfloat16),
        "col",
        scatter_dimension=0,
        tiled=True,
    )
    return (output, grad_tokens, grad_weight_in, grad_weight_out, grad_bias)


def solution(mesh):
    placed = (P("col", "row"), P("row", "col"), P("col", "row"), P("col"), P("col", "row"))
    return jax.shard_map(
        per_device,
        mesh=mesh,
        in_specs=placed,
        out_specs=(P("col", "row"), P("col", "row"), P("row", "col"), P("col", "row"), P("col")),
        check_vma=False,
    )
```

profile of v0, /device:TPU:0, one launch (start us, length us, event | category | flops | bytes accessed | tf_op | source)
XLA Modules:
  0.0 437.9 jit_solution(2398990751486347006)
XLA Ops:
  7.2 0.7 all-gather.9.cloned.1.call-update
  7.9 0.7 all-gather.5.cloned.1.call-update
  8.7 34.9 %all-gather.9.cloned.1.call-done = bf16[512,1536]{1,0:T(8,128)(2,1)} async-done(((bf16[128,1536]{1,0:T(8,128)(2,1)}), bf16[512,1536]{1,0:T(8,128)(2,1)}) %all-gather.9.cloned.1.call-update) | async-done | bytes 1572880 | tf_op jit(solution)/shard_map/all_gather | solution.py:69
  43.5 15.9 %convolution_convert_fusion = bf16[512,6144]{1,0:T(8,128)(2,1)} fusion(bf16[512,1536]{1,0:T(8,128)(2,1)} %all-gather.9.cloned.1.call-done, bf16[6144,1536]{1,0:T(8,128)(2,1)} %param.7), kind=kOutput, calls=%fused_computation.4 | convolution fusion | flops 9666822144 | bytes 26738688 | tf_op jit(solution)/shard_map/dot_general | solution.py:29
  59.5 0.0 reduce-scatter.5.cloned.1.call-start
  59.5 16.9 %all-gather.5.cloned.1.call-done = bf16[512,1536]{1,0:T(8,128)(2,1)} async-done(((bf16[128,1536]{1,0:T(8,128)(2,1)}), bf16[512,1536]{1,0:T(8,128)(2,1)}) %all-gather.5.cloned.1.call-update) | async-done | bytes 1572880 | tf_op jit(solution)/shard_map/all_gather | solution.py:45
  76.4 15.9 %convolution_convert_fusion.1 = bf16[512,6144]{1,0:T(8,128)(2,1)} fusion(bf16[512,1536]{1,0:T(8,128)(2,1)} %all-gather.5.cloned.1.call-done, bf16[1536,6144]{1,0:T(8,128)(2,1)} %param.6), kind=kOutput, calls=%fused_computation.5 | convolution fusion | flops 9666822144 | bytes 26738688 | tf_op jit(solution)/shard_map/dot_general | solution.py:49
  92.3 0.0 all-gather.7.cloned.1.call-start
  92.3 0.6 copy-done
  93.0 56.1 %reduce-scatter.9.cloned.1.call-done = bf16[64,6144]{1,0:T(8,128)(2,1)} async-done(((bf16[512,6144]{1,0:T(8,128)(2,1)}), bf16[64,6144]{1,0:T(8,128)(2,1)}) %reduce-scatter.9.cloned.1.call-update) | async-done | bytes 786448 | tf_op jit(solution)/shard_map/reduce_scatter | solution.py:71
  149.1 70.9 %reduce-scatter.5.cloned.1.call-done = bf16[64,6144]{1,0:T(8,128)(2,1)} async-done(((bf16[512,6144]{1,0:T(8,128)(2,1)}), bf16[64,6144]{1,0:T(8,128)(2,1)}) %reduce-scatter.5.cloned.1.call-update) | async-done | bytes 786448 | tf_op jit(solution)/shard_map/reduce_scatter | solution.py:48
  220.1 3.7 fusion.7
  223.9 0.5 all-gather.11.cloned.1.call-update
  224.4 0.2 reduce-scatter.7.cloned.1.call-start
  224.6 62.5 %all-gather.7.cloned.1.call-done = bf16[512,6144]{1,0:T(8,128)(2,1)} async-done(((bf16[64,6144]{1,0:T(8,128)(2,1)}), bf16[512,6144]{1,0:T(8,128)(2,1)}) %all-gather.7.cloned.1.call-update) | async-done | bytes 6291472 | tf_op jit(solution)/shard_map/all_gather | solution.py:59
  287.1 16.6 %convolution_convert_fusion.3 = bf16[512,1536]{1,0:T(8,128)(2,1)} fusion(bf16[512,6144]{1,0:T(8,128)(2,1)} %all-gather.7.cloned.1.call-done, bf16[6144,1536]{1,0:T(8,128)(2,1)} %param.7), kind=kOutput, calls=%fused_computation.7 | convolution fusion | flops 9664462848 | bytes 26738688 | tf_op jit(solution)/shard_map/dot_general | solution.py:62
  303.8 0.0 reduce-scatter.11.cloned.1.call-start
  303.8 48.8 %all-gather.11.cloned.1.call-done = bf16[512,6144]{1,0:T(8,128)(2,1)} async-done(((bf16[64,6144]{1,0:T(8,128)(2,1)}), bf16[512,6144]{1,0:T(8,128)(2,1)}) %all-gather.11.cloned.1.call-update) | async-done | bytes 6291472 | tf_op jit(solution)/shard_map/all_gather | solution.py:78
  352.6 16.6 %convolution_convert_fusion.2 = bf16[512,1536]{1,0:T(8,128)(2,1)} fusion(bf16[512,6144]{1,0:T(8,128)(2,1)} %all-gather.11.cloned.1.call-done, bf16[1536,6144]{1,0:T(8,128)(2,1)} %param.6), kind=kOutput, calls=%fused_computation.6 | convolution fusion | flops 9664462848 | bytes 26738688 | tf_op jit(solution)/shard_map/dot_general | solution.py:29
  369.2 16.0 %fusion = bf16[1536,6144]{0,1:T(8,128)(2,1)} fusion(bf16[512,6144]{1,0:T(8,128)(2,1)} %all-gather.11.cloned.1.call-done, bf16[512,1536]{1,0:T(8,128)(2,1)S(1)} %copy-done.2), kind=kOutput, calls=%fused_computation.2 | convolution fusion | flops 9682550784 | bytes 26738688 | tf_op jit(solution)/shard_map/dot_general | solution.py:35
  385.2 24.7 %copy.10 = bf16[1536,6144]{1,0:T(8,128)(2,1)} copy(bf16[1536,6144]{0,1:T(8,128)(2,1)} %fusion) | data formatting | bytes 37748736
  409.9 4.5 %convert_reduce_fusion = f32[6144]{0:T(1024)S(1)} fusion(bf16[512,6144]{1,0:T(8,128)(2,1)} %all-gather.11.cloned.1.call-done), kind=kLoop, calls=%fused_computation.3 | loop fusion | flops 6285312 | bytes 6316032 | tf_op jit(solution)/shard_map/reduce_sum | solution.py:81
  414.4 0.6 broadcast_multiply_fusion
  415.0 16.0 %multiply_convert_fusion = bf16[6144,1536]{1,0:T(8,128)(2,1)} fusion(bf16[512,6144]{1,0:T(8,128)(2,1)} %all-gather.7.cloned.1.call-done, bf16[512,1536]{1,0:T(8,128)(2,1)S(1)} %copy-done.1), kind=kOutput, calls=%fused_computation | convolution fusion | flops 9682550784 | bytes 26738688 | tf_op jit(solution)/shard_map/dot_general | solution.py:35
  (17 shorter events, 0.3 us)
Async XLA Ops:
  7.2 36.4 %all-gather.9.cloned.1.call-start = ((), (), s32[]{:S(2)}) async-start(), calls=%async_computation.8 | async-start | bytes 1966080 | tf_op jit(solution)/shard_map/all_gather | solution.py:69
  7.9 68.5 %all-gather.5.cloned.1.call-start = ((), (), s32[]{:S(2)}) async-start(), calls=%async_computation.4 | async-start | bytes 1966080 | tf_op jit(solution)/shard_map/all_gather | solution.py:45
  8.6 140.5 %reduce-scatter.9.cloned.1.call-start = ((), (), s32[]{:S(2)}) async-start(), calls=%async_computation.9 | async-start | bytes 7077888 | tf_op jit(solution)/shard_map/reduce_scatter | solution.py:71
  59.5 160.6 %reduce-scatter.5.cloned.1.call-start = ((), (), s32[]{:S(2)}) async-start(), calls=%async_computation.5 | async-start | bytes 7077888 | tf_op jit(solution)/shard_map/reduce_scatter | solution.py:48
  92.3 0.7 copy-start
  92.3 194.8 %all-gather.7.cloned.1.call-start = ((), (), s32[]{:S(2)}) async-start(), calls=%async_computation.6 | async-start | bytes 7077888 | tf_op jit(solution)/shard_map/all_gather | solution.py:59
  223.8 128.8 %all-gather.11.cloned.1.call-start = ((), (), s32[]{:S(2)}) async-start(), calls=%async_computation.10 | async-start | bytes 7077888 | tf_op jit(solution)/shard_map/all_gather | solution.py:78
  224.4 206.6 %reduce-scatter.7.cloned.1.call-start = ((), (), s32[]{:S(2)}) async-start(), calls=%async_computation.7 | async-start | bytes 1966080 | tf_op jit(solution)/shard_map/reduce_scatter | solution.py:61
  303.7 65.4 %copy-start.2 = (bf16[512,1536]{1,0:T(8,128)(2,1)S(1)}, bf16[512,1536]{1,0:T(8,128)(2,1)}, u32[]{:S(2)}) copy-start(bf16[512,1536]{1,0:T(8,128)(2,1)} %all-gather.5.cloned.1.call-done) | copy-start | bytes 4718596
  303.8 127.3 %reduce-scatter.11.cloned.1.call-start = ((), (), s32[]{:S(2)}) async-start(), calls=%async_computation.11 | async-start | bytes 1966080 | tf_op jit(solution)/shard_map/reduce_scatter | solution.py:83
  409.9 5.1 %copy-start.1 = (bf16[512,1536]{1,0:T(8,128)(2,1)S(1)}, bf16[512,1536]{1,0:T(8,128)(2,1)}, u32[]{:S(2)}) copy-start(bf16[512,1536]{1,0:T(8,128)(2,1)} %all-gather.9.cloned.1.call-done) | copy-start | bytes 4718596
Sparse Core Ops, SparseCore 0:
  9.8 33.6 all-gather.8
  45.4 30.9 all-gather.4
  79.3 69.7 reduce-scatter.8
  151.8 68.1 reduce-scatter.4
  223.9 63.1 all-gather.6
  289.2 63.3 all-gather.10
  356.2 29.5 reduce-scatter.6
  389.3 30.9 reduce-scatter.10
where the time goes:
time: 439 us; the launch traced here: 438 us
  waiting for transfers between devices  292 us (67%)
  matrix products  97 us (22%)
  local copies, waits for them, and re-layouts  25.3 us (6%)
  between operations  14.2 us (3%)
  other arithmetic  8.81 us (2%)
    reduce_scatter x1, waiting for transfers between devices, per_device(): lax.psum_scatter(rounded(jnp.dot(sliced, weight_in, preferred_element_typ...  70.9 us
    all_gather x1, waiting for transfers between devices, per_device(): hidden_all = lax.all_gather(hidden, 'row', axis=0, tiled=True)  62.5 us
    reduce_scatter x1, waiting for transfers between devices, per_device(): lax.psum_scatter(rounded(times_transposed(sliced, weight_out)).astype(jnp...  56.1 us
    all_gather x1, waiting for transfers between devices, per_device(): slope_all = lax.all_gather(slope_grad, 'row', axis=0, tiled=True)  48.8 us
    all_gather x1, waiting for transfers between devices, per_device(): cotangent_all = lax.all_gather(cotangent, 'col', axis=0, tiled=True)  34.9 us
    dot_general x2, matrix products, times_transposed(): lax.dot_general(left, right, (((1,), (1,)), ((), ())), preferred_element_...  32.5 us
    dot_general x2, matrix products, over_tokens(): lax.dot_general(left, right, (((0,), (0,)), ((), ())), preferred_element_...  32 us
    unnamed x7, local copies, waits for them, and re-layouts  25.3 us
  transfers between devices with their start and end apart: 8, of which 6 were waited for; matrix products, arithmetic and copies ran while one was open for 29% of the time, Pallas kernels for 0%

commit v1 on v0

v1 whole, which is shorter than its diff:
```python
import functools
import math

import jax
import jax.numpy as jnp
from jax import lax
from jax.experimental import pallas as pl
from jax.experimental.pallas import tpu as pltpu
from jax.sharding import PartitionSpec as P

gelu_coef = math.sqrt(2.0 / math.pi)
cubic_coef = 0.044715


def gelu_tanh(values):
    inner = jnp.tanh(gelu_coef * (values + cubic_coef * values * values * values))
    return 0.5 * values * (1.0 + inner)


def gelu_slope(values):
    inner = jnp.tanh(gelu_coef * (values + cubic_coef * values * values * values))
    return 0.5 * (1.0 + inner) + 0.5 * values * (1.0 - inner * inner) * gelu_coef * (
        1.0 + 3.0 * cubic_coef * values * values
    )


MESH = pl.DeviceIdType.MESH
wide = 256
row_step = 64


def over_tokens(left, right):
    return lax.dot_general(
        left, right, (((0,), (0,)), ((), ())), preferred_element_type=jnp.float32
    )


def times_transposed(left, right):
    return lax.dot_general(
        left, right, (((1,), (1,)), ((), ())), preferred_element_type=jnp.float32
    )


def times(left, right):
    return jnp.dot(left, right, preferred_element_type=jnp.float32)


def chain_kernel(
    length, parts, tok, cot, bias, win, wout, hid_o, slope_o, out_o, gt_o,
    gathered, sums, theirs, mine, near_in, near_out, far_in, far_out, acc_o, acc_g,
    sum_send, sum_recv, pair_send, pair_recv, ring_send, ring_recv, hand_send, hand_recv,
    near_sem, far_sem, store_sem,
):
    steps = 2 * parts
    count = tok.shape[0]
    depth = tok.shape[1]
    quarter = parts * wide
    place = lax.axis_index("row")
    spot = place // 2
    core = place % 2
    partner = spot * 2 + (1 - core)

    def device(other):
        return {"row": other}

    barrier = pltpu.get_barrier_semaphore()
    pl.semaphore_signal(barrier, inc=1, device_id=device(partner), device_id_type=MESH)

    @pl.when(spot > 0)
    def _():
        pl.semaphore_signal(barrier, inc=1, device_id=device(place - 2), device_id_type=MESH)

    @pl.when(spot < length - 1)
    def _():
        pl.semaphore_signal(barrier, inc=1, device_id=device(place + 2), device_id_type=MESH)

    acc_o[...] = jnp.zeros_like(acc_o)
    acc_g[...] = jnp.zeros_like(acc_g)

    pl.semaphore_wait(barrier, 1 + jnp.where(spot > 0, 1, 0) + jnp.where(spot < length - 1, 1, 0))

    def columns(q, part):
        return pl.ds(pl.multiple_of(q * quarter + part * wide, wide), wide)

    def load(q, part, from_in, in_slot, out_slot, sem):
        first = pltpu.make_async_copy(win.at[:, columns(q, part)], in_slot, sem)
        second = pltpu.make_async_copy(wout.at[columns(q, part), :], out_slot, sem)
        return first if from_in else second

    def near_quarter(item):
        way = item // 2
        own = item % 2
        return way, own, way * 2 + jnp.where(own == 1, core, 1 - core)

    def near_copy(item, step, from_in):
        way, own, q = near_quarter(item)
        return load(q, step % parts, from_in, near_in.at[item], near_out.at[item], near_sem.at[item])

    def far_copy(way, which, step, from_in):
        slot = way * 2 + which
        return load(slot, step % parts, from_in, far_in.at[slot], far_out.at[slot], far_sem.at[slot])

    def hops(way):
        return length - 1 - spot if way == 0 else spot

    def onward(way):
        return place - 2 if way == 0 else place + 2

    def backward(way):
        return place + 2 if way == 0 else place - 2

    def sum_copy(way, step):
        return pltpu.make_async_remote_copy(
            src_ref=sums.at[way, step], dst_ref=sums.at[way, step],
            send_sem=sum_send.at[way, step], recv_sem=sum_recv.at[way, step],
            device_id=device(onward(way)), device_id_type=MESH)

    def pair_copy(way, step):
        return pltpu.make_async_remote_copy(
            src_ref=mine.at[way, steps + step % 2], dst_ref=theirs.at[way, step],
            send_sem=pair_send.at[way, step % 2], recv_sem=pair_recv.at[way, step],
            device_id=device(partner), device_id_type=MESH)

    def ring_copy(way, step):
        return pltpu.make_async_remote_copy(
            src_ref=gathered.at[way * 2 + core, step], dst_ref=gathered.at[way * 2 + core, step],
            send_sem=ring_send.at[way, step], recv_sem=ring_recv.at[way, step],
            device_id=device(backward(way)), device_id_type=MESH)

    def hand_copy(way, step, q):
        return pltpu.make_async_remote_copy(
            src_ref=gathered.at[q, step], dst_ref=gathered.at[q, step],
            send_sem=hand_send.at[way, step], recv_sem=hand_recv.at[way, step],
            device_id=device(partner), device_id_type=MESH)

    def store_copy(q, step, is_hidden):
        target = hid_o if is_hidden else slope_o
        return pltpu.make_async_copy(
            gathered.at[q, step], target.at[:, columns(q, step % parts)], store_sem.at[q, step])

    def in_rows(body):
        def one(index, carry):
            body(pl.ds(pl.multiple_of(index * row_step, row_step), row_step))
            return carry

        lax.fori_loop(0, count // row_step, one, 0)

    def wide_of(ref, way, step, rows):
        return ref[way, step, rows, :].astype(jnp.float32)

    def combine(way, step, hop):
        pair_copy(way, step).wait_recv()

        @pl.when(hop == 0)
        def _():
            def body(rows):
                total = wide_of(mine, way, step, rows) + wide_of(theirs, way, step, rows)
                sums[way, step, rows, :] = total.astype(jnp.bfloat16)

            in_rows(body)

        @pl.when(hop > 0)
        def _():
            sum_copy(way, step).wait_recv()

        def total_of(at, rows):
            return (
                wide_of(mine, way, at, rows) + wide_of(theirs, way, at, rows)
            ) + wide_of(sums, way, at, rows)

        @pl.when(jnp.logical_and(hop > 0, hop < length - 1))
        def _():
            def body(rows):
                sums[way, step, rows, :] = total_of(step, rows).astype(jnp.bfloat16)

            in_rows(body)

        @pl.when(hop < length - 1)
        def _():
            sum_copy(way, step).start()

        @pl.when(hop == length - 1)
        def _():
            q = way * 2 + core
            shift = bias[q * parts + step % parts]

            @pl.when(step < parts)
            def _():
                def body(rows):
                    pre = total_of(step, rows) + shift
                    gathered[q, step, rows, :] = gelu_tanh(pre).astype(jnp.bfloat16)

                in_rows(body)

            @pl.when(step >= parts)
            def _():
                def body(rows):
                    pre = total_of(step - parts, rows) + shift
                    slope = total_of(step, rows) * gelu_slope(pre)
                    gathered[q, step, rows, :] = slope.astype(jnp.bfloat16)

                in_rows(body)

            ring_copy(way, step).start()
            hand_copy(way, step, q).start()

    def pass_on(way, step, hop):
        ring_copy(way, step).wait_recv()

        @pl.when(hop > 0)
        def _():
            ring_copy(way, step).start()

        hand_copy(way, step, way * 2 + core).start()

    def within(step):
        return jnp.logical_and(step >= 0, step < steps)

    def both_kinds(step, act):
        @pl.when(step < parts)
        def _():
            act(True)

        @pl.when(step >= parts)
        def _():
            act(False)

    def turn(now, carry):
        @pl.when(now < steps)
        def _():
            def start(item, inner):
                both_kinds(now, lambda first: near_copy(item, now, first).start())
                return inner

            lax.fori_loop(0, 4, start, 0)

        for way in range(2):
            used = now - 2 - 2 * (length - 1) + hops(way)

            @pl.when(within(used))
            def _(way=way, used=used):
                for which in range(2):
                    both_kinds(used, lambda first: far_copy(way, which, used, not first).start())

        for way in range(2):
            hop = hops(way)
            ready = now - 1 - hop

            @pl.when(within(ready))
            def _(way=way, ready=ready, hop=hop):
                combine(way, ready, hop)

            here = now - 1 - 2 * (length - 1) + hop

            @pl.when(jnp.logical_and(within(here), hop < length - 1))
            def _(way=way, here=here, hop=hop):
                pass_on(way, here, hop)

        @pl.when(now < steps)
        def _():
            def one(item, inner):
                way, own, _ = near_quarter(item)
                slot = jnp.where(own == 1, now, steps + now % 2)

                @pl.when(jnp.logical_and(own == 0, now >= 2))
                def _():
                    pair_copy(way, now).wait_send()

                @pl.when(now < parts)
                def _():
                    near_copy(item, now, True).wait()
                    mine[way, slot] = times(tok[...], near_in[item]).astype(jnp.bfloat16)

                @pl.when(now >= parts)
                def _():
                    near_copy(item, now, False).wait()
                    mine[way, slot] = times_transposed(cot[...], near_out[item]).astype(jnp.bfloat16)

                @pl.when(own == 0)
                def _():
                    pair_copy(way, now).start()

                return inner

            lax.fori_loop(0, 4, one, 0)

        def use(way, inner):
            hop = jnp.where(way == 0, hops(0), hops(1))
            used = now - 2 - 2 * (length - 1) + hop

            @pl.when(within(used))
            def _():
                hand_copy(way, used, way * 2 + 1 - core).wait_recv()
                for which in range(2):
                    both_kinds(used, lambda first: store_copy(way * 2 + which, used, first).start())
                slab = depth // 3

                @pl.when(used < parts)
                def _():
                    for which in range(2):
                        far_copy(way, which, used, False).wait()
                    for third in range(3):
                        at = slice(third * slab, (third + 1) * slab)
                        acc_o[:, at] += times(gathered[way * 2, used], far_out[way * 2, :, at]) + times(
                            gathered[way * 2 + 1, used], far_out[way * 2 + 1, :, at])

                @pl.when(used >= parts)
                def _():
                    for which in range(2):
                        far_copy(way, which, used, True).wait()
                    for third in range(3):
                        at = slice(third * slab, (third + 1) * slab)
                        acc_g[:, at] += times_transposed(
                            gathered[way * 2, used], far_in[way * 2, at, :]
                        ) + times_transposed(gathered[way * 2 + 1, used], far_in[way * 2 + 1, at, :])

            return inner

        lax.fori_loop(0, 2, use, 0)
        return carry

    lax.fori_loop(0, steps + 2 * length, turn, 0)
    out_o[...] = acc_o[...].astype(jnp.bfloat16)
    gt_o[...] = acc_g[...].astype(jnp.bfloat16)

    def finish(step, carry):
        for way in range(2):
            hop = hops(way)

            @pl.when(hop < length - 1)
            def _(way=way):
                sum_copy(way, step).wait_send()

            @pl.when(hop > 0)
            def _(way=way):
                ring_copy(way, step).wait_send()

            hand_copy(way, step, way * 2 + core).wait_send()
            for which in range(2):
                both_kinds(step, lambda first: store_copy(way * 2 + which, step, first).wait())
        return carry

    lax.fori_loop(0, steps, finish, 0)
    for way in range(2):
        for step in (steps - 2, steps - 1):
            pair_copy(way, step).wait_send()


def chain(length, tokens_all, cotangent_all, bias_wide, weight_in, weight_out):
    count, depth = tokens_all.shape
    hidden_units = weight_in.shape[1]
    parts = hidden_units // (4 * wide)
    steps = 2 * parts
    bf16 = jnp.bfloat16
    vmem = pl.BlockSpec(memory_space=pltpu.VMEM)
    anywhere = pl.BlockSpec(memory_space=pl.ANY)
    dma = pltpu.SemaphoreType.DMA
    return pl.pallas_call(
        functools.partial(chain_kernel, length, parts),
        out_shape=(
            jax.ShapeDtypeStruct((count, hidden_units), bf16),
            jax.ShapeDtypeStruct((count, hidden_units), bf16),
            jax.ShapeDtypeStruct((count, depth), bf16),
            jax.ShapeDtypeStruct((count, depth), bf16),
        ),
        in_specs=[vmem, vmem, vmem, anywhere, anywhere],
        out_specs=(anywhere, anywhere, vmem, vmem),
        scratch_shapes=[
            pltpu.VMEM((4, steps, count, wide), bf16),
            pltpu.VMEM((2, steps, count, wide), bf16),
            pltpu.VMEM((2, steps, count, wide), bf16),
            pltpu.VMEM((2, steps + 2, count, wide), bf16),
            pltpu.VMEM((4, depth, wide), bf16),
            pltpu.VMEM((4, wide, depth), bf16),
            pltpu.VMEM((4, depth, wide), bf16),
            pltpu.VMEM((4, wide, depth), bf16),
            pltpu.VMEM((count, depth), jnp.float32),
            pltpu.VMEM((count, depth), jnp.float32),
            dma((2, steps)), dma((2, steps)), dma((2, 2)), dma((2, steps)),
            dma((2, steps)), dma((2, steps)), dma((2, steps)), dma((2, steps)),
            dma((4,)), dma((4,)), dma((4, steps)),
        ],
        compiler_params=pltpu.CompilerParams(
            collective_id=0, has_side_effects=True, vmem_limit_bytes=60 * 1024 * 1024
        ),
    )(tokens_all, cotangent_all, bias_wide.reshape(-1, 1, wide), weight_in, weight_out)


def slope_kernel(factor, left, right, grad, total, turned):
    @pl.when(pl.program_id(0) == 0)
    def _():
        turned[...] = left[...].T

    grad[...] = (times(turned[...], right[...]) * factor).astype(jnp.bfloat16)
    total[...] = jnp.sum(right[...].astype(jnp.float32), axis=0, keepdims=True) * factor


def slope_grads(factor, left, right):
    count, depth = left.shape
    units = right.shape[1]
    block = 2 * wide
    return pl.pallas_call(
        functools.partial(slope_kernel, factor),
        grid=(units // block,),
        out_shape=(
            jax.ShapeDtypeStruct((depth, units), jnp.bfloat16),
            jax.ShapeDtypeStruct((1, units), jnp.float32),
        ),
        in_specs=[
            pl.BlockSpec((count, depth), lambda j: (0, 0)),
            pl.BlockSpec((count, block), lambda j: (0, j)),
        ],
        out_specs=(
            pl.BlockSpec((depth, block), lambda j: (0, j)),
            pl.BlockSpec((1, block), lambda j: (0, j)),
        ),
        scratch_shapes=[pltpu.VMEM((depth, count), jnp.bfloat16)],
        compiler_params=pltpu.CompilerParams(vmem_limit_bytes=40 * 1024 * 1024),
        cost_estimate=pl.CostEstimate(
            flops=2 * count * depth * units,
            bytes_accessed=2 * (count * depth + count * units + depth * units),
            transcendentals=0,
        ),
    )(left, right)


def per_device(length, tokens, weight_in, weight_out, bias_in, cotangent):
    rows_here = tokens.shape[0]
    total_rows = rows_here * lax.axis_size("col")
    factor = 1.0 / math.sqrt(total_rows)
    tokens_all = lax.all_gather(tokens, "col", axis=0, tiled=True)
    cotangent_all = lax.all_gather(cotangent, "col", axis=0, tiled=True)
    hidden_all, slope_all, output, grad_tokens = chain(
        length, tokens_all, cotangent_all, bias_in.astype(jnp.float32), weight_in, weight_out
    )
    output = lax.psum_scatter(output, "col", scatter_dimension=0, tiled=True)
    grad_tokens = lax.psum_scatter(grad_tokens, "col", scatter_dimension=0, tiled=True)
    grad_weight_out = (over_tokens(hidden_all, cotangent_all) * factor).astype(jnp.bfloat16)
    grad_weight_in, grad_bias = slope_grads(factor, tokens_all, slope_all)
    grad_bias = grad_bias.reshape(-1)
    return (output, grad_tokens, grad_weight_in, grad_weight_out, grad_bias)


def solution(mesh):
    placed = (P("col", "row"), P("row", "col"), P("col", "row"), P("col"), P("col", "row"))
    return jax.shard_map(
        functools.partial(per_device, mesh.shape["row"] // 2),
        mesh=mesh,
        in_specs=placed,
        out_specs=(P("col", "row"), P("col", "row"), P("row", "col"), P("col", "row"), P("col")),
        check_vma=False,
    )
```

time: 439 us -> 319 us (0.73)
  waiting for transfers between devices: 292 us -> 97 us
  Pallas kernels: 0 us -> 188 us
  matrix products: 97 us -> 16 us
  local copies, waits for them, and re-layouts: 25.3 us -> 2.79 us
  other arithmetic: 8.81 us -> 1.32 us
    pallas_call x0 -> x2, Pallas kernels: none -> 188 us  [the longest x1 173 us: chain(): pl.pallas_call(functools.partial(chain_kernel, length, parts), out_shape=...]
    all_gather x2 -> x0, waiting for transfers between devices: 111 us -> none  [the longest x1 62.5 us: per_device(): hidden_all = lax.all_gather(hidden, 'row', axis=0, tiled=True)]
    reduce_scatter x4 -> x2, waiting for transfers between devices: 127 us -> 28.7 us  [the longest x1 28.7 us: per_device(): lax.psum_scatter(grad_tokens, 'col', scatter_dimension=0, tiled=True)]
    dot_general x4 -> x0, matrix products: 64.9 us -> none  [the longest x2 32.5 us: times_transposed(): lax.dot_general(left, right, (((1,), (1,)), ((), ())), preferred_element_...]
    unnamed x7 -> x6, local copies, waits for them, and re-layouts: 25.3 us -> 2.79 us
    all_gather x1, waiting for transfers between devices: 16.9 us -> 33.5 us  [per_device(): tokens_all = lax.all_gather(tokens, 'col', axis=0, tiled=True)]
    dot_general x2 -> x1, matrix products: 32 us -> 16 us  [over_tokens(): lax.dot_general(left, right, (((0,), (0,)), ((), ())), preferred_element_...]
    reduce_sum x1 -> x0, other arithmetic: 4.47 us -> none  [per_device(): grad_bias = jnp.sum(slope_all, axis=0, dtype=jnp.float32) * factor]
  transfers between devices with their start and end apart: 8 -> 4, of which waited for: 6 -> 3; matrix products, arithmetic and copies ran while one was open for 29% -> 5% of each run, Pallas kernels for 0% -> 5%
where the time goes in v1:
time: 319 us
  Pallas kernels  188 us (59%)
  waiting for transfers between devices  97 us (30%)
  matrix products  16 us (5%)
  between operations  13.8 us (4%)
    pallas_call x1, Pallas kernels, chain(): pl.pallas_call(functools.partial(chain_kernel, length, parts), out_shape=...  173 us
    all_gather x1, waiting for transfers between devices, per_device(): tokens_all = lax.all_gather(tokens, 'col', axis=0, tiled=True)  33.5 us
    all_gather x1, waiting for transfers between devices, per_device(): cotangent_all = lax.all_gather(cotangent, 'col', axis=0, tiled=True)  32.8 us
    reduce_scatter x1, waiting for transfers between devices, per_device(): lax.psum_scatter(grad_tokens, 'col', scatter_dimension=0, tiled=True)  28.7 us
    dot_general x1, matrix products, over_tokens(): lax.dot_general(left, right, (((0,), (0,)), ((), ())), preferred_element_...  16 us
    pallas_call x1, Pallas kernels, slope_grads(): pl.pallas_call(functools.partial(slope_kernel, factor), grid=(units // bl...  14.6 us
  transfers between devices with their start and end apart: 4, of which 3 were waited for; matrix products, arithmetic and copies ran while one was open for 5% of the time, Pallas kernels for 5%

profile of v1, /device:TPU:0, one launch (start us, length us, event | category | flops | bytes accessed | tf_op | source)
XLA Modules:
  0.0 318.9 jit_solution(9654080958860428351)
XLA Ops:
  7.2 0.0 all-gather.3.cloned.1.call-start
  7.2 0.7 all-gather.3.cloned.1.call-update
  7.9 0.0 all-gather.5.cloned.1.call-start
  7.9 0.7 all-gather.5.cloned.1.call-update
  8.7 0.0 reduce-scatter.3.cloned.1.call-start
  8.7 1.3 reshape.21
  10.0 33.5 %all-gather.3.cloned.1.call-done.tok.left = bf16[512,1536]{1,0:T(8,128)(2,1)} async-done(((bf16[128,1536]{1,0:T(8,128)(2,1)}), bf16[512,1536]{1,0:T(8,128)(2,1)}) %all-gather.3.cloned.1.call-update) | async-done | bytes 1572880 | tf_op jit(solution)/shard_map/all_gather | solution.py:431
  43.6 32.8 %all-gather.5.cloned.1.call-done.cot = bf16[512,1536]{1,0:T(8,128)(2,1)} async-done(((bf16[128,1536]{1,0:T(8,128)(2,1)}), bf16[512,1536]{1,0:T(8,128)(2,1)}) %all-gather.5.cloned.1.call-update) | async-done | bytes 1572880 | tf_op jit(solution)/shard_map/all_gather | solution.py:432
  76.4 0.0 copy-start
  76.4 173.2 %shard_map.92 = (bf16[512,6144]{1,0:T(8,128)(2,1)}, bf16[512,6144]{1,0:T(8,128)(2,1)}, bf16[512,1536]{1,0:T(8,128)(2,1)}, bf16[512,1536]{1,0:T(8,128)(2,1)}) custom-call(bf16[512,1536]{1,0:T(8,128)(2,1)} %all-gather.3.cloned.1.call-done.tok.left, bf16[512,1536]{1,0:T(8,128)(2,1)} %all-gather.5.cloned.1.call-done.cot, f32[24,1,256]{2,1,0:T(1,128)} %bitcast.4, ...), custom_call_target="tpu_custom_call" | custom-call | tf_op jit(solution)/shard_map/pallas_call | solution.py:358
  249.7 0.0 reduce-scatter.3.cloned.1.call-update
  249.7 0.0 reduce-scatter.5.cloned.1.call-start
  249.7 0.5 reduce-scatter.5.cloned.1.call-update
  250.3 0.0 copy-done
  250.3 0.0 copy-start.1
  250.3 2.8 copy-done.1
  253.1 0.0 copy-start.2
  253.1 14.6 %shard_map.93 = (bf16[1536,6144]{1,0:T(8,128)(2,1)}, f32[1,6144]{1,0:T(1,128)}) custom-call(bf16[512,1536]{1,0:T(8,128)(2,1)S(1)} %copy-done, bf16[512,6144]{1,0:T(8,128)(2,1)S(1)} %copy-done.1), custom_call_target="tpu_custom_call" | custom-call | flops 9663676416 | bytes 26738688 | tf_op jit(solution)/shard_map/pallas_call | solution.py:402
  267.7 0.0 copy-done.2
  267.7 16.0 %multiply_convert_fusion = bf16[6144,1536]{1,0:T(8,128)(2,1)} fusion(bf16[512,6144]{1,0:T(8,128)(2,1)} %get-tuple-element.15, bf16[512,1536]{1,0:T(8,128)(2,1)S(1)} %copy-done.2), kind=kOutput, calls=%fused_computation | convolution fusion | flops 9682550784 | bytes 26738688 | tf_op jit(solution)/shard_map/dot_general | solution.py:33
  283.7 0.0 reduce-scatter.3.cloned.1.call-done
  283.7 28.7 %reduce-scatter.5.cloned.1.call-done = bf16[128,1536]{1,0:T(8,128)(2,1)} async-done(((bf16[512,1536]{1,0:T(8,128)(2,1)}), bf16[128,1536]{1,0:T(8,128)(2,1)}) %reduce-scatter.5.cloned.1.call-update) | async-done | bytes 393232 | tf_op jit(solution)/shard_map/reduce_scatter | solution.py:437
Async XLA Ops:
  7.2 36.4 %all-gather.3.cloned.1.call-start = ((), (), s32[]{:S(2)}) async-start(), calls=%async_computation.2 | async-start | bytes 1966080 | tf_op jit(solution)/shard_map/all_gather | solution.py:431
  7.9 68.5 %all-gather.5.cloned.1.call-start = ((), (), s32[]{:S(2)}) async-start(), calls=%async_computation.3 | async-start | bytes 1966080 | tf_op jit(solution)/shard_map/all_gather | solution.py:432
  8.7 275.0 %reduce-scatter.3.cloned.1.call-start = ((), (), s32[]{:S(2)}) async-start(), calls=%async_computation.4 | async-start | bytes 1966080 | tf_op jit(solution)/shard_map/reduce_scatter | solution.py:436
  76.4 173.9 %copy-start = (bf16[512,1536]{1,0:T(8,128)(2,1)S(1)}, bf16[512,1536]{1,0:T(8,128)(2,1)}, u32[]{:S(2)}) copy-start(bf16[512,1536]{1,0:T(8,128)(2,1)} %all-gather.3.cloned.1.call-done.tok.left) | copy-start | bytes 4718596
  249.7 62.7 %reduce-scatter.5.cloned.1.call-start = ((), (), s32[]{:S(2)}) async-start(), calls=%async_computation.5 | async-start | bytes 1966080 | tf_op jit(solution)/shard_map/reduce_scatter | solution.py:437
  250.3 2.8 copy-start.1
  253.1 14.6 %copy-start.2 = (bf16[512,1536]{1,0:T(8,128)(2,1)S(1)}, bf16[512,1536]{1,0:T(8,128)(2,1)}, u32[]{:S(2)}) copy-start(bf16[512,1536]{1,0:T(8,128)(2,1)} %all-gather.5.cloned.1.call-done.cot) | copy-start | bytes 4718596
Sparse Core Ops, SparseCore 0:
  9.8 33.6 all-gather.2
  45.4 30.9 all-gather.4
  249.8 28.1 reduce-scatter.2
  281.4 30.9 reduce-scatter.4

commit v2 on v1

--- a/solution.py
+++ b/solution.py
@@ -46,10 +46,10 @@
 
 
 def chain_kernel(
-    length, parts, tok, cot, bias, win, wout, hid_o, slope_o, out_o, gt_o,
-    gathered, sums, theirs, mine, near_in, near_out, far_in, far_out, acc_o, acc_g,
+    length, groups, parts, tok_here, cot_here, bias, win, wout, hid_o, slope_o, out_o, gt_o, tok_o, cot_o,
+    tok, cot, staged, landed, gathered, sums, theirs, mine, near_in, near_out, far_in, far_out, acc_o, acc_g,
     sum_send, sum_recv, pair_send, pair_recv, ring_send, ring_recv, hand_send, hand_recv,
-    near_sem, far_sem, store_sem,
+    near_sem, far_sem, store_sem, own_sem, whole_sem, share_send, share_recv, out_send, out_recv,
 ):
     steps = 2 * parts
     count = tok.shape[0]
@@ -59,12 +59,55 @@
     spot = place // 2
     core = place % 2
     partner = spot * 2 + (1 - core)
+    group = lax.axis_index("col")
+    rows_each = count // groups
+
+    def peer(offset):
+        return lax.rem(group + offset + groups, groups)
+
+    def rows_of(which):
+        return pl.ds(pl.multiple_of(which * rows_each, rows_each), rows_each)
+
+    def own_copy(kind):
+        source, target = ((tok_here, tok), (cot_here, cot))[kind]
+        return pltpu.make_async_copy(source, target.at[rows_of(group), :], own_sem.at[kind])
+
+    def whole_copy(kind):
+        source, target = ((tok, tok_o), (cot, cot_o))[kind]
+        return pltpu.make_async_copy(source, target, whole_sem.at[kind])
+
+    def share_copy(kind, offset, rows):
+        ref = (tok, cot)[kind]
+        return pltpu.make_async_remote_copy(
+            src_ref=ref.at[rows_of(rows), :], dst_ref=ref.at[rows_of(rows), :],
+            send_sem=share_send.at[kind, offset], recv_sem=share_recv.at[kind, offset],
+            device_id={"col": peer(offset)}, device_id_type=MESH)
+
+    def share(kind):
+        for offset in range(1, groups):
+            share_copy(kind, offset, group).start()
+
+    def shared(kind):
+        for offset in range(1, groups):
+            share_copy(kind, offset, peer(-offset)).wait_recv()
+        whole_copy(kind).start()
+
+    def out_copy(offset):
+        return pltpu.make_async_remote_copy(
+            src_ref=staged.at[rows_of(peer(offset)), :], dst_ref=landed.at[offset - 1],
+            send_sem=out_send.at[offset], recv_sem=out_recv.at[offset],
+            device_id={"col": peer(offset)}, device_id_type=MESH)
+
+    own_copy(0).start()
+    own_copy(1).start()
 
     def device(other):
         return {"row": other}
 
     barrier = pltpu.get_barrier_semaphore()
     pl.semaphore_signal(barrier, inc=1, device_id=device(partner), device_id_type=MESH)
+    for offset in range(1, groups):
+        pl.semaphore_signal(barrier, inc=1, device_id={"col": peer(offset)}, device_id_type=MESH)
 
     @pl.when(spot > 0)
     def _():
@@ -74,10 +117,15 @@
     def _():
         pl.semaphore_signal(barrier, inc=1, device_id=device(place + 2), device_id_type=MESH)
 
+    own_copy(0).wait()
+    own_copy(1).wait()
+    pl.semaphore_wait(barrier, groups + jnp.where(spot > 0, 1, 0) + jnp.where(spot < length - 1, 1, 0))
+
+    share(0)
     acc_o[...] = jnp.zeros_like(acc_o)
     acc_g[...] = jnp.zeros_like(acc_g)
-
-    pl.semaphore_wait(barrier, 1 + jnp.where(spot > 0, 1, 0) + jnp.where(spot < length - 1, 1, 0))
+    shared(0)
+    share(1)
 
     def columns(q, part):
         return pl.ds(pl.multiple_of(q * quarter + part * wide, wide), wide)
@@ -250,11 +298,9 @@
             def _(way=way, ready=ready, hop=hop):
                 combine(way, ready, hop)
 
-            here = now - 1 - 2 * (length - 1) + hop
-
-            @pl.when(jnp.logical_and(within(here), hop < length - 1))
-            def _(way=way, here=here, hop=hop):
-                pass_on(way, here, hop)
+        @pl.when(now == parts)
+        def _():
+            shared(1)
 
         @pl.when(now < steps)
         def _():
@@ -283,6 +329,14 @@
                 return inner
 
             lax.fori_loop(0, 4, one, 0)
+
+        for way in range(2):
+            hop = hops(way)
+            here = now - 1 - 2 * (length - 1) + hop
+
+            @pl.when(jnp.logical_and(within(here), hop < length - 1))
+            def _(way=way, here=here, hop=hop):
+                pass_on(way, here, hop)
 
         def use(way, inner):
             hop = jnp.where(way == 0, hops(0), hops(1))
@@ -317,10 +371,22 @@
             return inner
 
         lax.fori_loop(0, 2, use, 0)
+
+        @pl.when(now == parts - 1 + 2 * length)
+        def _():
+            staged[...] = acc_o[...].astype(jnp.bfloat16)
+            for offset in range(1, groups):
+                out_copy(offset).start()
+
         return carry
 
     lax.fori_loop(0, steps + 2 * length, turn, 0)
-    out_o[...] = acc_o[...].astype(jnp.bfloat16)
+    for offset in range(1, groups):
+        out_copy(offset).wait_recv()
+    total = acc_o[rows_of(group), :]
+    for offset in range(1, groups):
+        total = total + landed[offset - 1].astype(jnp.float32)
+    out_o[...] = total.astype(jnp.bfloat16)
     gt_o[...] = acc_g[...].astype(jnp.bfloat16)
 
     def finish(step, carry):
@@ -341,13 +407,20 @@
         return carry
 
     lax.fori_loop(0, steps, finish, 0)
+    for kind in range(2):
+        whole_copy(kind).wait()
+        for offset in range(1, groups):
+            share_copy(kind, offset, group).wait_send()
+    for offset in range(1, groups):
+        out_copy(offset).wait_send()
     for way in range(2):
         for step in (steps - 2, steps - 1):
             pair_copy(way, step).wait_send()
 
 
-def chain(length, tokens_all, cotangent_all, bias_wide, weight_in, weight_out):
-    count, depth = tokens_all.shape
+def chain(length, groups, tokens, cotangent, bias_wide, weight_in, weight_out):
+    rows_each, depth = tokens.shape
+    count = rows_each * groups
     hidden_units = weight_in.shape[1]
     parts = hidden_units // (4 * wide)
     steps = 2 * parts
@@ -356,16 +429,22 @@
     anywhere = pl.BlockSpec(memory_space=pl.ANY)
     dma = pltpu.SemaphoreType.DMA
     return pl.pallas_call(
-        functools.partial(chain_kernel, length, parts),
+        functools.partial(chain_kernel, length, groups, parts),
         out_shape=(
             jax.ShapeDtypeStruct((count, hidden_units), bf16),
             jax.ShapeDtypeStruct((count, hidden_units), bf16),
+            jax.ShapeDtypeStruct((rows_each, depth), bf16),
+            jax.ShapeDtypeStruct((count, depth), bf16),
             jax.ShapeDtypeStruct((count, depth), bf16),
             jax.ShapeDtypeStruct((count, depth), bf16),
         ),
-        in_specs=[vmem, vmem, vmem, anywhere, anywhere],
-        out_specs=(anywhere, anywhere, vmem, vmem),
+        in_specs=[anywhere, anywhere, vmem, anywhere, anywhere],
+        out_specs=(anywhere, anywhere, vmem, vmem, anywhere, anywhere),
         scratch_shapes=[
+            pltpu.VMEM((count, depth), bf16),
+            pltpu.VMEM((count, depth), bf16),
+            pltpu.VMEM((count, depth), bf16),
+            pltpu.VMEM((groups - 1, rows_each, depth), bf16),
             pltpu.VMEM((4, steps, count, wide), bf16),
             pltpu.VMEM((2, steps, count, wide), bf16),
             pltpu.VMEM((2, steps, count, wide), bf16),
@@ -379,11 +458,12 @@
             dma((2, steps)), dma((2, steps)), dma((2, 2)), dma((2, steps)),
             dma((2, steps)), dma((2, steps)), dma((2, steps)), dma((2, steps)),
             dma((4,)), dma((4,)), dma((4, steps)),
+            dma((2,)), dma((2,)), dma((2, groups)), dma((2, groups)), dma((groups,)), dma((groups,)),
         ],
         compiler_params=pltpu.CompilerParams(
-            collective_id=0, has_side_effects=True, vmem_limit_bytes=60 * 1024 * 1024
+            collective_id=0, has_side_effects=True, vmem_limit_bytes=61 * 1024 * 1024
         ),
-    )(tokens_all, cotangent_all, bias_wide.reshape(-1, 1, wide), weight_in, weight_out)
+    )(tokens, cotangent, bias_wide.reshape(-1, 1, wide), weight_in, weight_out)
 
 
 def slope_kernel(factor, left, right, grad, total, turned):
@@ -424,16 +504,13 @@
     )(left, right)
 
 
-def per_device(length, tokens, weight_in, weight_out, bias_in, cotangent):
+def per_device(length, groups, tokens, weight_in, weight_out, bias_in, cotangent):
     rows_here = tokens.shape[0]
     total_rows = rows_here * lax.axis_size("col")
     factor = 1.0 / math.sqrt(total_rows)
-    tokens_all = lax.all_gather(tokens, "col", axis=0, tiled=True)
-    cotangent_all = lax.all_gather(cotangent, "col", axis=0, tiled=True)
-    hidden_all, slope_all, output, grad_tokens = chain(
-        length, tokens_all, cotangent_all, bias_in.astype(jnp.float32), weight_in, weight_out
+    hidden_all, slope_all, output, grad_tokens, tokens_all, cotangent_all = chain(
+        length, groups, tokens, cotangent, bias_in.astype(jnp.float32), weight_in, weight_out
     )
-    output = lax.psum_scatter(output, "col", scatter_dimension=0, tiled=True)
     grad_tokens = lax.psum_scatter(grad_tokens, "col", scatter_dimension=0, tiled=True)
     grad_weight_out = (over_tokens(hidden_all, cotangent_all) * factor).astype(jnp.bfloat16)
     grad_weight_in, grad_bias = slope_grads(factor, tokens_all, slope_all)
@@ -444,7 +521,7 @@
 def solution(mesh):
     placed = (P("col", "row"), P("row", "col"), P("col", "row"), P("col"), P("col", "row"))
     return jax.shard_map(
-        functools.partial(per_device, mesh.shape["row"] // 2),
+        functools.partial(per_device, mesh.shape["row"] // 2, mesh.shape["col"]),
         mesh=mesh,
         in_specs=placed,
         out_specs=(P("col", "row"), P("col", "row"), P("row", "col"), P("col", "row"), P("col")),

time: 319 us -> 242 us (0.76)
  waiting for transfers between devices: 97 us -> 0.02 us
  Pallas kernels: 188 us -> 208 us
    all_gather x2 -> x0, waiting for transfers between devices: 66.4 us -> none  [the longest x1 33.5 us: per_device(): tokens_all = lax.all_gather(tokens, 'col', axis=0, tiled=True)]
    reduce_scatter x1, waiting for transfers between devices: 28.7 us -> 0.01 us  [per_device(): lax.psum_scatter(grad_tokens, 'col', scatter_dimension=0, tiled=True)]
    pallas_call x1, Pallas kernels: 173 us -> 194 us  [chain(): pl.pallas_call(functools.partial(chain_kernel, length, groups, parts), ou...]
  transfers between devices with their start and end apart: 4 -> 1, of which waited for: 3 -> 0; matrix products, arithmetic and copies ran while one was open for 5% -> 5% of each run, Pallas kernels for 5% -> 6%
where the time goes in v2:
time: 242 us
  Pallas kernels  208 us (86%)
  between operations  14.1 us (6%)
  matrix products  13.3 us (5%)
  local copies, waits for them, and re-layouts  4.94 us (2%)
    pallas_call x1, Pallas kernels, chain(): pl.pallas_call(functools.partial(chain_kernel, length, groups, parts), ou...  194 us
    pallas_call x1, Pallas kernels, slope_grads(): pl.pallas_call(functools.partial(slope_kernel, factor), grid=(units // bl...  14.6 us
    dot_general x1, matrix products, over_tokens(): lax.dot_general(left, right, (((0,), (0,)), ((), ())), preferred_element_...  13.3 us
    unnamed x11, local copies, waits for them, and re-layouts  4.94 us
  transfers between devices with their start and end apart: 1, of which 0 were waited for; matrix products, arithmetic and copies ran while one was open for 5% of the time, Pallas kernels for 6%

profile of v2, /device:TPU:0, one launch (start us, length us, event | category | flops | bytes accessed | tf_op | source)
XLA Modules:
  0.0 241.8 jit_solution(16479422160601730390)
XLA Ops:
  7.2 0.0 reduce-scatter.2.cloned.1.call-start
  7.2 1.3 reshape.21
  8.5 193.5 %shard_map.92 = (bf16[512,6144]{1,0:T(8,128)(2,1)}, bf16[512,6144]{1,0:T(8,128)(2,1)}, bf16[128,1536]{1,0:T(8,128)(2,1)}, bf16[512,1536]{1,0:T(8,128)(2,1)}, bf1...) custom-call(bf16[128,1536]{1,0:T(8,128)(2,1)} %tok_here.1, bf16[128,1536]{1,0:T(8,128)(2,1)} %cot_here.1, ...), custom_call_target="tpu_custom_call" | custom-call | tf_op jit(solution)/shard_map/pallas_call | solution.py:431
  202.1 0.0 reduce-scatter.2.cloned.1.call-update
  202.1 0.0 copy-start
  202.1 2.8 %copy-done = bf16[512,6144]{1,0:T(8,128)(2,1)S(1)} copy-done((bf16[512,6144]{1,0:T(8,128)(2,1)S(1)}, bf16[512,6144]{1,0:T(8,128)(2,1)}, u32[]{:S(2)}) %copy-start) | copy-done | bytes 6291480
  204.9 0.0 copy-start.1
  204.9 1.4 copy-done.1
  206.3 0.0 copy-start.3
  206.3 0.0 copy-start.4
  206.3 14.6 %shard_map.93 = (bf16[1536,6144]{1,0:T(8,128)(2,1)}, f32[1,6144]{1,0:T(1,128)}) custom-call(bf16[512,1536]{1,0:T(8,128)(2,1)S(1)} %copy-done.1, bf16[512,6144]{1,0:T(8,128)(2,1)S(1)} %copy-done), custom_call_target="tpu_custom_call" | custom-call | flops 9663676416 | bytes 26738688 | tf_op jit(solution)/shard_map/pallas_call | solution.py:482
  220.9 0.0 copy-done.3
  220.9 0.0 copy-done.4
  220.9 0.0 copy-start.2
  220.9 13.3 %multiply_convert_fusion = bf16[6144,1536]{1,0:T(8,128)(2,1)} fusion(bf16[512,6144]{1,0:T(8,128)(2,1)S(1)} %copy-done.3, bf16[512,1536]{1,0:T(8,128)(2,1)S(1)} %copy-done.4), kind=kOutput, calls=%fused_computation | convolution fusion | flops 9682550784 | bytes 26738688 | tf_op jit(solution)/shard_map/dot_general | solution.py:33
  234.2 0.0 reduce-scatter.2.cloned.1.call-done
  234.2 0.0 copy-done.2
  234.2 0.7 copy.11
Async XLA Ops:
  7.2 227.0 %reduce-scatter.2.cloned.1.call-start = ((), (), s32[]{:S(2)}) async-start(), calls=%async_computation.1 | async-start | bytes 1966080 | tf_op jit(solution)/shard_map/reduce_scatter | solution.py:514
  202.1 2.8 %copy-start = (bf16[512,6144]{1,0:T(8,128)(2,1)S(1)}, bf16[512,6144]{1,0:T(8,128)(2,1)}, u32[]{:S(2)}) copy-start(bf16[512,6144]{1,0:T(8,128)(2,1)} %get-tuple-element.16.right) | copy-start | bytes 18874372
  204.9 1.4 copy-start.1
  206.3 14.6 %copy-start.3 = (bf16[512,6144]{1,0:T(8,128)(2,1)S(1)}, bf16[512,6144]{1,0:T(8,128)(2,1)}, u32[]{:S(2)}) copy-start(bf16[512,6144]{1,0:T(8,128)(2,1)} %get-tuple-element.18) | copy-start | bytes 18874372
  206.3 14.6 %copy-start.4 = (bf16[512,1536]{1,0:T(8,128)(2,1)S(1)}, bf16[512,1536]{1,0:T(8,128)(2,1)}, u32[]{:S(2)}) copy-start(bf16[512,1536]{1,0:T(8,128)(2,1)} %get-tuple-element.19) | copy-start | bytes 4718596
  220.9 13.3 %copy-start.2 = (bf16[128,1536]{1,0:T(8,128)(2,1)S(1)}, bf16[128,1536]{1,0:T(8,128)(2,1)}, u32[]{:S(2)}) copy-start(bf16[128,1536]{1,0:T(8,128)(2,1)} %get-tuple-element.26) | copy-start | bytes 1179652
Sparse Core Ops, SparseCore 0:
  202.2 30.4 reduce-scatter.1

commit v3 on v2

--- a/solution.py
+++ b/solution.py
@@ -27,12 +27,6 @@
 MESH = pl.DeviceIdType.MESH
 wide = 256
 row_step = 64
-
-
-def over_tokens(left, right):
-    return lax.dot_general(
-        left, right, (((0,), (0,)), ((), ())), preferred_element_type=jnp.float32
-    )
 
 
 def times_transposed(left, right):
@@ -495,7 +489,33 @@
             pl.BlockSpec((1, block), lambda j: (0, j)),
         ),
         scratch_shapes=[pltpu.VMEM((depth, count), jnp.bfloat16)],
-        compiler_params=pltpu.CompilerParams(vmem_limit_bytes=40 * 1024 * 1024),
+        compiler_params=pltpu.CompilerParams(vmem_limit_bytes=60 * 1024 * 1024),
+        cost_estimate=pl.CostEstimate(
+            flops=2 * count * depth * units,
+            bytes_accessed=2 * (count * depth + count * units + depth * units),
+            transcendentals=0,
+        ),
+    )(left, right)
+
+
+def hidden_kernel(factor, left, right, grad):
+    grad[...] = (times(left[...].T, right[...]) * factor).astype(jnp.bfloat16)
+
+
+def hidden_grads(factor, left, right):
+    count, units = left.shape
+    depth = right.shape[1]
+    block = 2 * wide
+    return pl.pallas_call(
+        functools.partial(hidden_kernel, factor),
+        grid=(units // block,),
+        out_shape=jax.ShapeDtypeStruct((units, depth), jnp.bfloat16),
+        in_specs=[
+            pl.BlockSpec((count, block), lambda j: (0, j)),
+            pl.BlockSpec((count, depth), lambda j: (0, 0)),
+        ],
+        out_specs=pl.BlockSpec((block, depth), lambda j: (j, 0)),
+        compiler_params=pltpu.CompilerParams(vmem_limit_bytes=60 * 1024 * 1024),
         cost_estimate=pl.CostEstimate(
             flops=2 * count * depth * units,
             bytes_accessed=2 * (count * depth + count * units + depth * units),
@@ -512,7 +532,7 @@
         length, groups, tokens, cotangent, bias_in.astype(jnp.float32), weight_in, weight_out
     )
     grad_tokens = lax.psum_scatter(grad_tokens, "col", scatter_dimension=0, tiled=True)
-    grad_weight_out = (over_tokens(hidden_all, cotangent_all) * factor).astype(jnp.bfloat16)
+    grad_weight_out = hidden_grads(factor, hidden_all, cotangent_all)
     grad_weight_in, grad_bias = slope_grads(factor, tokens_all, slope_all)
     grad_bias = grad_bias.reshape(-1)
     return (output, grad_tokens, grad_weight_in, grad_weight_out, grad_bias)

time: 242 us -> 246 us (1.017)
  Pallas kernels: 208 us -> 229 us
  matrix products: 13.3 us -> 0 us
  local copies, waits for them, and re-layouts: 4.94 us -> 0.75 us
    pallas_call x0 -> x1, Pallas kernels: none -> 17.4 us  [hidden_grads(): pl.pallas_call(functools.partial(hidden_kernel, factor), grid=(units // b...]
    dot_general x1 -> x0, matrix products: 13.3 us -> none  [over_tokens(): lax.dot_general(left, right, (((0,), (0,)), ((), ())), preferred_element_...]
    unnamed x11 -> x3, local copies, waits for them, and re-layouts: 4.94 us -> 0.75 us
    pallas_call x1, Pallas kernels: 14.6 us -> 18 us  [slope_grads(): pl.pallas_call(functools.partial(slope_kernel, factor), grid=(units // bl...]
  transfers between devices with their start and end apart: 1 -> 1, of which waited for: 0 -> 0; matrix products, arithmetic and copies ran while one was open for 5% -> 0% of each run, Pallas kernels for 6% -> 14%
where the time goes in v3:
time: 246 us; the launch traced here: 245 us
  Pallas kernels  229 us (93%)
  between operations  14 us (6%)
    pallas_call x1, Pallas kernels, chain(): pl.pallas_call(functools.partial(chain_kernel, length, groups, parts), ou...  194 us
    pallas_call x1, Pallas kernels, slope_grads(): pl.pallas_call(functools.partial(slope_kernel, factor), grid=(units // bl...  18 us
    pallas_call x1, Pallas kernels, hidden_grads(): pl.pallas_call(functools.partial(hidden_kernel, factor), grid=(units // b...  17.4 us
  transfers between devices with their start and end apart: 1, of which 0 were waited for; matrix products, arithmetic and copies ran while one was open for 0% of the time, Pallas kernels for 14%

profile of v3, /device:TPU:0, one launch (start us, length us, event | category | flops | bytes accessed | tf_op | source)
XLA Modules:
  0.0 245.1 jit_solution(10189555506926493723)
XLA Ops:
  7.2 0.0 reduce-scatter.2.cloned.1.call-start
  7.2 1.3 reshape.21
  8.5 193.6 %shard_map.92 = (bf16[512,6144]{1,0:T(8,128)(2,1)}, bf16[512,6144]{1,0:T(8,128)(2,1)}, bf16[128,1536]{1,0:T(8,128)(2,1)}, bf16[512,1536]{1,0:T(8,128)(2,1)}, bf1...) custom-call(bf16[128,1536]{1,0:T(8,128)(2,1)} %tok_here.1, bf16[128,1536]{1,0:T(8,128)(2,1)} %cot_here.1, ...), custom_call_target="tpu_custom_call" | custom-call | tf_op jit(solution)/shard_map/pallas_call | solution.py:425
  202.1 0.0 reduce-scatter.2.cloned.1.call-update
  202.1 17.4 %shard_map.94 = bf16[6144,1536]{1,0:T(8,128)(2,1)} custom-call(bf16[512,6144]{1,0:T(8,128)(2,1)} %get-tuple-element.18.left, bf16[512,1536]{1,0:T(8,128)(2,1)} %get-tuple-element.19.right), custom_call_target="tpu_custom_call" | custom-call | flops 9663676416 | bytes 26738688 | tf_op jit(solution)/shard_map/pallas_call | solution.py:509
  219.6 0.0 copy-start
  219.6 18.0 %shard_map.93 = (bf16[1536,6144]{1,0:T(8,128)(2,1)}, f32[1,6144]{1,0:T(1,128)}) custom-call(bf16[512,1536]{1,0:T(8,128)(2,1)} %get-tuple-element.15.left, bf16[512,6144]{1,0:T(8,128)(2,1)} %get-tuple-element.16.right), custom_call_target="tpu_custom_call" | custom-call | flops 9663676416 | bytes 26738688 | tf_op jit(solution)/shard_map/pallas_call | solution.py:476
  237.5 0.0 reduce-scatter.2.cloned.1.call-done
  237.5 0.0 copy-done
  237.5 0.7 copy.11
Async XLA Ops:
  7.2 230.4 %reduce-scatter.2.cloned.1.call-start = ((), (), s32[]{:S(2)}) async-start(), calls=%async_computation.1 | async-start | bytes 1966080 | tf_op jit(solution)/shard_map/reduce_scatter | solution.py:534
  219.6 18.0 %copy-start = (bf16[128,1536]{1,0:T(8,128)(2,1)S(1)}, bf16[128,1536]{1,0:T(8,128)(2,1)}, u32[]{:S(2)}) copy-start(bf16[128,1536]{1,0:T(8,128)(2,1)} %get-tuple-element.26) | copy-start | bytes 1179652
Sparse Core Ops, SparseCore 0:
  202.2 30.4 reduce-scatter.1
